TPU v7x, 512 devices: a whole 4x8x8 slice. The times are simulated.
512 devices in a mesh: dp: 32 (over z, x_hi, core), comp: 16 (over x_lo, y).
Axes of the slice: x: 4 (x_hi: 2, x_lo: 2; x = x_hi * 2 + x_lo), y: 8, z: 8, core: 2. Of those that a mesh axis runs over, the one named last changes fastest.
Arguments:
- embeddings: float32 [32768, 768], P('dp'), may hold values from -6 to 6
- comp_means: float32 [8192, 768], P(('comp', 'dp')), may hold values from -1.2 to 1.2
- comp_variances: float32 [8192, 768], P(('comp', 'dp')), may hold values from 0.8 to 1.25
- comp_mass: float32 [8192], P(('comp', 'dp')), may hold values from 0.3 to 3
Outputs:
- new_means: float32 [8192, 768], P(('comp', 'dp'))
- new_variances: float32 [8192, 768], P(('comp', 'dp'))
- new_mass: float32 [8192], P(('comp', 'dp'))
All inputs are finite; a program needn't handle non-finite values.
Results may differ from a plain program's by a relative error of at most 0.0003.
Values sent between devices are 32-bit elements; how exact they have to be, the bound alone decides.
A program may use at most 64 MiB of HBM per device.

v0:
```python
import jax
import jax.numpy as jnp
from jax import lax
from jax.sharding import PartitionSpec as P


def coefficients(comp_means, comp_variances, comp_mass):
    precision = 1.0 / comp_variances
    neg_half = -0.5 * precision
    mean_prec = comp_means * precision
    offset = jnp.log(comp_mass) - 0.5 * jnp.sum(
        jnp.log(comp_variances) + comp_means * mean_prec, axis=1
    )
    return (neg_half, mean_prec, offset)


def moments_of(responsibility, values):
    return lax.dot_general(
        responsibility,
        values,
        (((0,), (0,)), ((), ())),
        precision=lax.Precision.HIGHEST,
        preferred_element_type=jnp.float32,
    )


def per_device(embeddings, comp_means, comp_variances, comp_mass):
    highest = lax.Precision.HIGHEST
    squares = embeddings * embeddings
    piece_half, piece_prec, piece_offset = coefficients(
        lax.all_gather(comp_means, "dp", axis=0, tiled=True),
        lax.all_gather(comp_variances, "dp", axis=0, tiled=True),
        lax.all_gather(comp_mass, "dp", axis=0, tiled=True),
    )
    quad = jnp.dot(squares, piece_half.T, precision=highest, preferred_element_type=jnp.float32)
    linear = jnp.dot(
        embeddings, piece_prec.T, precision=highest, preferred_element_type=jnp.float32
    )
    scores = quad + linear + piece_offset[None, :]
    local_peak = jnp.max(scores, axis=1)
    row_peak = lax.pmax(local_peak, "comp")
    shifted = jnp.exp(scores - row_peak[:, None])
    row_total = lax.psum(jnp.sum(shifted, axis=1), "comp")
    responsibility = shifted / row_total[:, None]
    first_sums = moments_of(responsibility, embeddings)
    second_sums = moments_of(responsibility, squares)
    counts = jnp.sum(responsibility, axis=0)
    first_sums, second_sums, counts = (
        lax.psum_scatter(first_sums, "dp", scatter_dimension=0, tiled=True),
        lax.psum_scatter(second_sums, "dp", scatter_dimension=0, tiled=True),
        lax.psum_scatter(counts, "dp", scatter_dimension=0, tiled=True),
    )
    total_comps = comp_means.shape[0] * lax.axis_size("dp") * lax.axis_size("comp")
    total_rows = embeddings.shape[0] * lax.axis_size("dp")
    mass_scale = total_comps / total_rows
    new_mass = 0.4 * comp_mass + 0.6 * mass_scale * counts
    first_moment = 0.4 * comp_mass[:, None] * comp_means + 0.6 * mass_scale * first_sums
    second_moment = (
        0.4 * comp_mass[:, None] * (comp_variances + comp_means * comp_means)
        + 0.6 * mass_scale * second_sums
    )
    new_means = first_moment / new_mass[:, None]
    new_variances = second_moment / new_mass[:, None] - new_means * new_means
    return (new_means, new_variances, new_mass)


def solution(mesh):
    placed = (P("dp", None), P(("comp", "dp"), None), P(("comp", "dp"), None), P(("comp", "dp")))
    return jax.shard_map(
        per_device,
        mesh=mesh,
        in_specs=placed,
        out_specs=(P(("comp", "dp"), None), P(("comp", "dp"), None), P(("comp", "dp"))),
        check_vma=False,
    )
```

profile of v0, /device:TPU:8, one launch (start us, length us, event | category | flops | bytes accessed | tf_op | source)
XLA Modules:
  0.0 530.1 jit_solution(17203534192863885605)
XLA Ops:
  7.2 0.0 all-gather.3.cloned.1.call-start
  7.2 0.7 all-gather.3.cloned.1.call-update
  7.9 0.0 all-gather.5.cloned.1.call-start
  7.9 0.7 all-gather.5.cloned.1.call-update
  8.6 0.0 reduce-scatter.3.cloned.1.call-start
  8.7 1.4 fusion.21
  10.7 0.9 dynamic-update-slice
  11.6 76.0 %all-reduce = f32[512]{0:T(512)S(1)} all-reduce(f32[512]{0:T(512)S(1)} %dynamic-update-slice), channel_id=1, replica_groups=mesh['dp'=32,'comp'=16] {'dp'}, use_global_device_ids=true, to_apply=%add | all-reduce | flops 512 | bytes 4096
  87.6 13.2 %all-gather.3.cloned.1.call-done = f32[512,768]{1,0:T(8,128)} async-done(((f32[16,768]{1,0:T(8,128)}), f32[512,768]{1,0:T(8,128)}) %all-gather.3.cloned.1.call-update) | async-done | bytes 1572880 | tf_op jit(solution)/shard_map/all_gather | solution.py:32
  100.8 0.0 copy-start
  100.8 84.3 %all-gather.5.cloned.1.call-done = f32[512,768]{1,0:T(8,128)} async-done(((f32[16,768]{1,0:T(8,128)}), f32[512,768]{1,0:T(8,128)}) %all-gather.5.cloned.1.call-update) | async-done | bytes 1572880 | tf_op jit(solution)/shard_map/all_gather | solution.py:31
  185.1 0.0 copy-start.2
  185.1 2.6 add_reduce_fusion
  187.7 0.0 copy-done
  187.7 0.0 copy-done.2
  187.7 0.0 copy-start.1
  187.7 0.0 copy-start.3
  187.7 7.3 %fusion.10 = f32[512,1024]{1,0:T(8,128)S(1)} fusion(f32[1024,768]{1,0:T(8,128)} %param.4, f32[512,768]{1,0:T(8,128)S(1)} %copy-done.2, f32[512,768]{1,0:T(8,128)S(1)} %copy-done), kind=kOutput, calls=%fused_computation.11 | convolution fusion | flops 4832624640 | bytes 8388608 | tf_op jit(solution)/shard_map/dot_general | solution.py:36
  195.0 0.0 copy-done.1
  195.0 0.0 copy-done.3
  195.0 5.4 %fusion.22 = (f32[1024]{0:T(1024)S(1)}, f32[1024,512]{0,1:T(8,128)S(1)}) fusion(f32[512]{0:T(512)S(1)} %multiply_subtract_fusion.1, f32[512,1024]{1,0:T(8,128)S(1)} %fusion.10, f32[512,768]{1,0:T(8,128)S(1)} %copy-done.1, f32[1024,768]{1,0:T(8,128)S(1)} %copy-done.3), kind=kOutput, calls=%fused_computation.27 | convolution fusion | flops 4834982912 | bytes 8919040 | tf_op jit(solution)/shard_map/dot_general | solution.py:35
  200.4 31.3 %pmax.7 = f32[1024]{0:T(1024)S(1)} all-reduce(f32[1024]{0:T(1024)S(1)} %get-tuple-element.9), channel_id=1, replica_groups=mesh['dp'=32,'comp'=16] {'comp'}, use_global_device_ids=true, to_apply=%region_2.0 | all-reduce | flops 1024 | bytes 8192 | tf_op jit(solution)/shard_map/pmax | solution.py:41
  231.7 0.3 fusion.6
  232.1 33.5 %psum.7 = f32[1024]{0:T(1024)S(1)} all-reduce(f32[1024]{0:T(1024)S(1)} %fusion.6), channel_id=1, replica_groups=mesh['dp'=32,'comp'=16] {'comp'}, use_global_device_ids=true, to_apply=%region_4.0 | all-reduce | flops 1024 | bytes 8192 | tf_op jit(solution)/shard_map/psum | solution.py:43
  265.5 8.4 %fusion.19 = f32[512,768]{1,0:T(8,128)} fusion(f32[1024,768]{1,0:T(8,128)} %param.4, f32[1024,512]{0,1:T(8,128)S(1)} %get-tuple-element.10, f32[1024]{0:T(1024)S(1)} %psum.7, f32[1024]{0:T(1024)S(1)} %pmax.7), kind=kOutput, calls=%fused_computation.25 | convolution fusion | flops 4832886784 | bytes 6823936 | tf_op jit(solution)/shard_map/dot_general | solution.py:18
  274.0 0.0 reduce-scatter.3.cloned.1.call-update
  274.0 0.0 reduce-scatter.5.cloned.1.call-start
  274.0 8.5 %fusion = f32[512,768]{1,0:T(8,128)} fusion(f32[1024,768]{1,0:T(8,128)} %param.4, f32[1024,512]{0,1:T(8,128)S(1)} %get-tuple-element.10, f32[1024]{0:T(1024)S(1)} %psum.7, f32[1024]{0:T(1024)S(1)} %pmax.7), kind=kOutput, calls=%fused_computation | convolution fusion | flops 4833673216 | bytes 6823936 | tf_op jit(solution)/shard_map/dot_general | solution.py:18
  282.5 0.0 copy-start.7
  282.5 0.0 copy-start.4
  282.5 0.0 copy-start.5
  282.5 0.0 reduce-scatter.5.cloned.1.call-update
  283.2 0.4 fusion.18
  283.6 65.1 %all-reduce.1 = f32[512]{0:T(512)S(1)} all-reduce(f32[512]{0:T(512)S(1)} %fusion.18), channel_id=3, replica_groups=mesh['dp'=32,'comp'=16] {'dp'}, use_global_device_ids=true, to_apply=%region_7.0.clone | all-reduce | flops 512 | bytes 4096
  348.8 0.0 copy-done.7
  348.8 0.1 broadcast_multiply_fusion
  348.9 0.0 copy-start.6
  348.9 44.6 %reduce-scatter.3.cloned.1.call-done = f32[16,768]{1,0:T(8,128)} async-done(((f32[512,768]{1,0:T(8,128)}), f32[16,768]{1,0:T(8,128)}) %reduce-scatter.3.cloned.1.call-update) | async-done | bytes 49168 | tf_op jit(solution)/shard_map/reduce_scatter | solution.py:49
  393.5 128.5 %reduce-scatter.5.cloned.1.call-done = f32[16,768]{1,0:T(8,128)} async-done(((f32[512,768]{1,0:T(8,128)}), f32[16,768]{1,0:T(8,128)}) %reduce-scatter.5.cloned.1.call-update) | async-done | bytes 49168 | tf_op jit(solution)/shard_map/reduce_scatter | solution.py:50
  522.0 0.0 copy-done.4
  522.0 0.0 copy-done.5
  522.0 1.5 multiply_subtract_fusion
  523.5 0.0 copy-done.6
  (2 shorter events, 0.0 us)
Async XLA Ops:
  7.2 93.6 %all-gather.3.cloned.1.call-start = ((), (), s32[]{:S(2)}) async-start(), calls=%async_computation.2 | async-start | bytes 1622016 | tf_op jit(solution)/shard_map/all_gather | solution.py:32
  7.9 177.2 %all-gather.5.cloned.1.call-start = ((), (), s32[]{:S(2)}) async-start(), calls=%async_computation.3 | async-start | bytes 1622016 | tf_op jit(solution)/shard_map/all_gather | solution.py:31
  8.6 384.8 %reduce-scatter.3.cloned.1.call-start = ((), (), s32[]{:S(2)}) async-start(), calls=%async_computation.4 | async-start | bytes 1622016 | tf_op jit(solution)/shard_map/reduce_scatter | solution.py:49
  100.8 86.9 %copy-start = (f32[512,768]{1,0:T(8,128)S(1)}, f32[512,768]{1,0:T(8,128)}, u32[]{:S(2)}) copy-start(f32[512,768]{1,0:T(8,128)} %all-gather.3.cloned.1.call-done) | copy-start | bytes 4718596
  185.1 2.6 copy-start.2
  187.7 7.3 %copy-start.1 = (f32[512,768]{1,0:T(8,128)S(1)}, f32[512,768]{1,0:T(8,128)}, u32[]{:S(2)}) copy-start(f32[512,768]{1,0:T(8,128)} %all-gather.3.cloned.1.call-done) | copy-start | bytes 4718596
  187.7 7.3 %copy-start.3 = (f32[1024,768]{1,0:T(8,128)S(1)}, f32[1024,768]{1,0:T(8,128)}, u32[]{:S(2)}) copy-start(f32[1024,768]{1,0:T(8,128)} %param.4) | copy-start | bytes 9437188
  274.0 248.0 %reduce-scatter.5.cloned.1.call-start = ((), (), s32[]{:S(2)}) async-start(), calls=%async_computation.5 | async-start | bytes 1622016 | tf_op jit(solution)/shard_map/reduce_scatter | solution.py:50
  282.5 66.3 %copy-start.7 = (f32[16]{0:T(128)S(1)}, f32[16]{0:T(128)}, u32[]{:S(2)}) copy-start(f32[16]{0:T(128)} %param.7) | copy-start | bytes 196
  282.5 239.5 %copy-start.4 = (f32[16,768]{1,0:T(8,128)S(1)}, f32[16,768]{1,0:T(8,128)}, u32[]{:S(2)}) copy-start(f32[16,768]{1,0:T(8,128)} %param.6) | copy-start | bytes 147460
  282.5 239.5 %copy-start.5 = (f32[16,768]{1,0:T(8,128)S(1)}, f32[16,768]{1,0:T(8,128)}, u32[]{:S(2)}) copy-start(f32[16,768]{1,0:T(8,128)} %param.5) | copy-start | bytes 147460
  348.9 174.7 %copy-start.6 = (f32[16]{0:T(128)}, f32[16]{0:T(128)S(1)}, u32[]{:S(2)}) copy-start(f32[16]{0:T(128)S(1)} %get-tuple-element.8) | copy-start | bytes 196
Sparse Core Ops, SparseCore 0:
  11.4 89.3 all-gather.2
  104.2 80.8 all-gather.4
  274.1 119.3 reduce-scatter.2
  398.0 123.9 reduce-scatter.4
where the time goes:
time: 530 us
  waiting for transfers between devices  272 us (51%)
  blocking collectives  206 us (39%)
  matrix products  29.6 us (6%)
  between operations  15.2 us (3%)
    unnamed x2, blocking collectives  141 us
    reduce_scatter x1, waiting for transfers between devices, per_device(): lax.psum_scatter(second_sums, 'dp', scatter_dimension=0, tiled=True)  129 us
    all_gather x1, waiting for transfers between devices, per_device(): lax.all_gather(comp_means, 'dp', axis=0, tiled=True)  84.3 us
    reduce_scatter x1, waiting for transfers between devices, per_device(): lax.psum_scatter(first_sums, 'dp', scatter_dimension=0, tiled=True)  44.6 us
    psum x1, blocking collectives, per_device(): row_total = lax.psum(jnp.sum(shifted, axis=1), 'comp')  33.5 us
    pmax x1, blocking collectives, per_device(): row_peak = lax.pmax(local_peak, 'comp')  31.3 us
    dot_general x2, matrix products, moments_of(): lax.dot_general(responsibility, values, (((0,), (0,)), ((), ())), precisi...  16.9 us
    all_gather x1, waiting for transfers between devices, per_device(): lax.all_gather(comp_variances, 'dp', axis=0, tiled=True)  13.2 us
  transfers between devices with their start and end apart: 4, of which 4 were waited for; matrix products, arithmetic and copies ran while one was open for 2% of the time, Pallas kernels for 0%

commit v1 on v0

--- a/solution.py
+++ b/solution.py
@@ -28,7 +28,9 @@
     highest = lax.Precision.HIGHEST
     squares = embeddings * embeddings
     piece_half, piece_prec, piece_offset = coefficients(
-        lax.all_gather(comp_means, "dp", axis=0, tiled=True),
+        jnp.concatenate(
+            lax.all_to_all(jnp.stack([comp_means] * lax.psum(1, "dp"), axis=0), "dp", 0, 0), 0
+        ),
         lax.all_gather(comp_variances, "dp", axis=0, tiled=True),
         lax.all_gather(comp_mass, "dp", axis=0, tiled=True),
     )

time: 530 us -> 467 us (0.88)
  waiting for transfers between devices: 272 us -> 179 us
  blocking collectives: 206 us -> 224 us
  starting transfers between devices: 0.16 us -> 13.3 us
    all_gather x1 -> x0, waiting for transfers between devices: 84.3 us -> none  [per_device(): lax.all_gather(comp_means, 'dp', axis=0, tiled=True)]
    unnamed x2, blocking collectives: 141 us -> 159 us
    all_gather x1, waiting for transfers between devices: 13.2 us -> 0.01 us  [per_device(): lax.all_gather(comp_variances, 'dp', axis=0, tiled=True)]
    all_to_all x0 -> x1, starting transfers between devices: none -> 13.2 us  [per_device(): lax.all_to_all(jnp.stack([comp_means] * lax.psum(1, 'dp'), axis=0), 'dp',...]
  transfers between devices with their start and end apart: 4 -> 4, of which waited for: 4 -> 2; matrix products, arithmetic and copies ran while one was open for 2% -> 3% of each run, Pallas kernels for 0% -> 0%
where the time goes in v1:
time: 467 us
  blocking collectives  224 us (48%)
  waiting for transfers between devices  179 us (38%)
  matrix products  27.6 us (6%)
  between operations  15.2 us (3%)
  starting transfers between devices  13.3 us (3%)
  other arithmetic  4.69 us (1%)
    unnamed x2, blocking collectives  159 us
    reduce_scatter x1, waiting for transfers between devices, per_device(): lax.psum_scatter(second_sums, 'dp', scatter_dimension=0, tiled=True)  129 us
    reduce_scatter x1, waiting for transfers between devices, per_device(): lax.psum_scatter(first_sums, 'dp', scatter_dimension=0, tiled=True)  49.3 us
    psum x1, blocking collectives, per_device(): row_total = lax.psum(jnp.sum(shifted, axis=1), 'comp')  33.5 us
    pmax x1, blocking collectives, per_device(): row_peak = lax.pmax(local_peak, 'comp')  31.9 us
    dot_general x2, matrix products, moments_of(): lax.dot_general(responsibility, values, (((0,), (0,)), ((), ())), precisi...  16.9 us
    all_to_all x1, starting transfers between devices, per_device(): lax.all_to_all(jnp.stack([comp_means] * lax.psum(1, 'dp'), axis=0), 'dp',...  13.2 us
  transfers between devices with their start and end apart: 4, of which 2 were waited for; matrix products, arithmetic and copies ran while one was open for 3% of the time, Pallas kernels for 0%

profile of v1, /device:TPU:8, one launch (start us, length us, event | category | flops | bytes accessed | tf_op | source)
XLA Modules:
  0.0 466.8 jit_solution(10426564410813477094)
XLA Ops:
  7.2 0.0 all-gather.2.cloned.1.call-start
  7.2 0.7 all-gather.2.cloned.1.call-update
  7.9 0.0 copy-start.5
  7.9 0.0 copy-start.6
  7.9 2.1 stack.2
  10.1 13.2 %all-to-all-start = ((f32[32,16,768]{2,1,0:T(8,128)}), f32[32,16,768]{2,1,0:T(8,128)S(1)}, u32[]{:S(2)}, u32[]{:S(2)}) async-start(f32[32,16,768]{2,1,0:T(8,128)} %stack.2), calls=%async_computation | async-start | bytes 3145728 | tf_op jit(solution)/shard_map/all_to_all | solution.py:32
  23.2 0.0 reduce-scatter.3.cloned.1.call-start
  23.3 0.0 copy-done.5
  23.3 0.6 fusion.20
  24.5 0.0 copy-done.6
  24.6 0.2 dynamic-update-slice
  24.8 93.9 %all-reduce = f32[512]{0:T(512)S(1)} all-reduce(f32[512]{0:T(512)S(1)} %dynamic-update-slice), channel_id=1, replica_groups=mesh['dp'=32,'comp'=16] {'dp'}, use_global_device_ids=true, to_apply=%add | all-reduce | flops 512 | bytes 4096
  118.7 0.0 all-gather.2.cloned.1.call-done
  118.7 0.0 all-to-all-done
  118.7 0.0 copy-start
  118.7 2.3 fusion.10
  121.0 0.0 copy-done
  121.1 0.0 copy-start.1
  121.1 5.3 %fusion.22 = f32[512,1024]{1,0:T(8,128)S(1)} fusion(f32[512,768]{1,0:T(8,128)S(1)} %get-tuple-element.6, f32[1024,768]{1,0:T(8,128)S(1)} %copy-done), kind=kOutput, calls=%fused_computation.28 | convolution fusion | flops 4831838208 | bytes 6815744 | tf_op jit(solution)/shard_map/dot_general | solution.py:38
  126.3 0.0 copy-done.1
  126.3 5.4 %fusion.21 = (f32[1024]{0:T(1024)S(1)}, f32[1024,512]{0,1:T(8,128)S(1)}) fusion(f32[512]{0:T(512)S(1)} %multiply_subtract_fusion.1, f32[512,1024]{1,0:T(8,128)S(1)} %fusion.22, f32[512,768]{1,0:T(8,128)S(1)} %copy-done.1, f32[1024,768]{1,0:T(8,128)S(1)} %copy-done), kind=kOutput, calls=%fused_computation.27 | convolution fusion | flops 4834982912 | bytes 8919040 | tf_op jit(solution)/shard_map/dot_general | solution.py:37
  131.8 31.9 %pmax.7 = f32[1024]{0:T(1024)S(1)} all-reduce(f32[1024]{0:T(1024)S(1)} %get-tuple-element.11), channel_id=1, replica_groups=mesh['dp'=32,'comp'=16] {'comp'}, use_global_device_ids=true, to_apply=%region_2.0 | all-reduce | flops 1024 | bytes 8192 | tf_op jit(solution)/shard_map/pmax | solution.py:43
  163.7 0.3 fusion.6
  164.0 33.5 %psum.7 = f32[1024]{0:T(1024)S(1)} all-reduce(f32[1024]{0:T(1024)S(1)} %fusion.6), channel_id=1, replica_groups=mesh['dp'=32,'comp'=16] {'comp'}, use_global_device_ids=true, to_apply=%region_4.0 | all-reduce | flops 1024 | bytes 8192 | tf_op jit(solution)/shard_map/psum | solution.py:45
  197.5 8.4 %fusion.18 = f32[512,768]{1,0:T(8,128)} fusion(f32[1024,768]{1,0:T(8,128)} %param.4, f32[1024,512]{0,1:T(8,128)S(1)} %get-tuple-element.12, f32[1024]{0:T(1024)S(1)} %psum.7, f32[1024]{0:T(1024)S(1)} %pmax.7), kind=kOutput, calls=%fused_computation.25 | convolution fusion | flops 4832886784 | bytes 6823936 | tf_op jit(solution)/shard_map/dot_general | solution.py:18
  205.9 0.0 reduce-scatter.3.cloned.1.call-update
  206.0 0.0 reduce-scatter.5.cloned.1.call-start
  206.0 8.5 %fusion = f32[512,768]{1,0:T(8,128)} fusion(f32[1024,768]{1,0:T(8,128)} %param.4, f32[1024,512]{0,1:T(8,128)S(1)} %get-tuple-element.12, f32[1024]{0:T(1024)S(1)} %psum.7, f32[1024]{0:T(1024)S(1)} %pmax.7), kind=kOutput, calls=%fused_computation | convolution fusion | flops 4833673216 | bytes 6823936 | tf_op jit(solution)/shard_map/dot_general | solution.py:18
  214.5 0.0 copy-start.2
  214.5 0.0 copy-start.3
  214.5 0.0 reduce-scatter.5.cloned.1.call-update
  215.2 0.4 fusion.17
  215.6 65.1 %all-reduce.1 = f32[512]{0:T(512)S(1)} all-reduce(f32[512]{0:T(512)S(1)} %fusion.17), channel_id=3, replica_groups=mesh['dp'=32,'comp'=16] {'dp'}, use_global_device_ids=true, to_apply=%region_7.0.clone | all-reduce | flops 512 | bytes 4096
  280.7 0.1 broadcast_multiply_fusion
  280.8 0.0 copy-start.4
  280.8 49.3 %reduce-scatter.3.cloned.1.call-done = f32[16,768]{1,0:T(8,128)} async-done(((f32[512,768]{1,0:T(8,128)}), f32[16,768]{1,0:T(8,128)}) %reduce-scatter.3.cloned.1.call-update) | async-done | bytes 49168 | tf_op jit(solution)/shard_map/reduce_scatter | solution.py:51
  330.2 128.5 %reduce-scatter.5.cloned.1.call-done = f32[16,768]{1,0:T(8,128)} async-done(((f32[512,768]{1,0:T(8,128)}), f32[16,768]{1,0:T(8,128)}) %reduce-scatter.5.cloned.1.call-update) | async-done | bytes 49168 | tf_op jit(solution)/shard_map/reduce_scatter | solution.py:52
  458.7 0.0 copy-done.2
  458.7 0.0 copy-done.3
  458.7 1.5 multiply_subtract_fusion
  460.2 0.0 copy-done.4
  (2 shorter events, 0.0 us)
Async XLA Ops:
  7.2 111.5 %all-gather.2.cloned.1.call-start = ((), (), s32[]{:S(2)}) async-start(), calls=%async_computation.3 | async-start | bytes 1622016 | tf_op jit(solution)/shard_map/all_gather | solution.py:34
  7.9 15.4 %copy-start.5 = (u32[512]{0:T(512)S(1)}, u32[512]{0:T(512)}, u32[]{:S(2)}) copy-start(u32[512]{0:T(512)} %constant.21) | copy-start | bytes 6148
  7.9 16.6 %copy-start.6 = (f32[16]{0:T(128)S(1)}, f32[16]{0:T(128)}, u32[]{:S(2)}) copy-start(f32[16]{0:T(128)} %param.7) | copy-start | bytes 196
  10.1 108.6 %all-to-all-start = ((f32[32,16,768]{2,1,0:T(8,128)}), f32[32,16,768]{2,1,0:T(8,128)S(1)}, u32[]{:S(2)}, u32[]{:S(2)}) async-start(f32[32,16,768]{2,1,0:T(8,128)} %stack.2), calls=%async_computation | async-start | bytes 3145728 | tf_op jit(solution)/shard_map/all_to_all | solution.py:32
  23.2 306.9 %reduce-scatter.3.cloned.1.call-start = ((), (), s32[]{:S(2)}) async-start(), calls=%async_computation.4 | async-start | bytes 1622016 | tf_op jit(solution)/shard_map/reduce_scatter | solution.py:51
  118.7 2.4 copy-start
  121.1 5.3 %copy-start.1 = (f32[512,768]{1,0:T(8,128)S(1)}, f32[512,768]{1,0:T(8,128)}, u32[]{:S(2)}) copy-start(f32[512,768]{1,0:T(8,128)} %all-gather.2.cloned.1.call-done) | copy-start | bytes 4718596
  206.0 252.7 %reduce-scatter.5.cloned.1.call-start = ((), (), s32[]{:S(2)}) async-start(), calls=%async_computation.5 | async-start | bytes 1622016 | tf_op jit(solution)/shard_map/reduce_scatter | solution.py:52
  214.5 244.2 %copy-start.2 = (f32[16,768]{1,0:T(8,128)S(1)}, f32[16,768]{1,0:T(8,128)}, u32[]{:S(2)}) copy-start(f32[16,768]{1,0:T(8,128)} %param.5) | copy-start | bytes 147460
  214.5 244.2 %copy-start.3 = (f32[16,768]{1,0:T(8,128)S(1)}, f32[16,768]{1,0:T(8,128)}, u32[]{:S(2)}) copy-start(f32[16,768]{1,0:T(8,128)} %param.6) | copy-start | bytes 147460
  280.8 179.4 %copy-start.4 = (f32[16]{0:T(128)}, f32[16]{0:T(128)S(1)}, u32[]{:S(2)}) copy-start(f32[16]{0:T(128)S(1)} %get-tuple-element.10) | copy-start | bytes 196
Sparse Core Ops, SparseCore 0:
  11.4 94.6 all-gather.1
  206.1 124.0 reduce-scatter.2
  334.9 123.7 reduce-scatter.4
